TPU v7x, 256 devices: a whole 4x4x8 slice. The times are simulated.
256 devices in a mesh: dp: 32 (over z_lo, y, core), fsdp: 8 (over z_hi, x).
Axes of the slice: x: 4, y: 4, z: 8 (z_hi: 2, z_lo: 4; z = z_hi * 4 + z_lo), core: 2. Of those that a mesh axis runs over, the one named last changes fastest.
Arguments:
- clip: bfloat16 [1, 128, 256, 1024], P(None, 'dp', 'fsdp'), may hold values from -6 to 6
- space_gain: float32 [1024], replicated, may hold values from 0.5 to 1.5
- space_qkv: bfloat16 [1024, 3072], P('fsdp'), may hold values from -2 to 2
- space_out: bfloat16 [1024, 1024], P('fsdp'), may hold values from -0.1875 to 0.1875
- mlp_gain: float32 [1024], replicated, may hold values from 0.5 to 1.5
- mlp_up: bfloat16 [1024, 4096], P('fsdp'), may hold values from -0.1875 to 0.1875
- mlp_down: bfloat16 [4096, 1024], P('fsdp'), may hold values from -0.09375 to 0.09375
- time_gain: float32 [1024], replicated, may hold values from 0.5 to 1.5
- time_qkv: bfloat16 [1024, 3072], P('fsdp'), may hold values from -2 to 2
- time_out: bfloat16 [1024, 1024], P('fsdp'), may hold values from -0.1875 to 0.1875
Outputs:
- encoded: bfloat16 [1, 128, 256, 1024], P(None, 'dp', 'fsdp')
All inputs are finite; a program needn't handle non-finite values.
Results may differ from a plain program's by a relative error of at most 0.017.
Values may be sent and summed in bfloat16 or wider, within the bound.
No kernel may reach another device: no remote copies, remote signals or barrier semaphores. Data moves between devices by JAX's collectives and lax.ppermute only.
A program may use at most 128 MiB of HBM per device.

v0:
```python
import jax
import jax.numpy as jnp
from jax import lax
from jax.sharding import PartitionSpec as P

HEADS = 16


def layer_norm(values, gain):
    wide = values.astype(jnp.float32)
    centre = jnp.mean(wide, axis=-1, keepdims=True)
    spread = jnp.mean((wide - centre) * (wide - centre), axis=-1, keepdims=True)
    return ((wide - centre) * lax.rsqrt(spread + 1e-06) * gain).astype(jnp.bfloat16)


def heads_attend(query, keys, values):
    batch, length, width = query.shape
    span = keys.shape[1]
    head_size = width // HEADS
    query_heads = query.reshape(batch, length, HEADS, head_size)
    key_heads = keys.reshape(batch, span, HEADS, head_size)
    value_heads = values.reshape(batch, span, HEADS, head_size)
    scores = jnp.einsum(
        "bqhd,bkhd->bhqk", query_heads, key_heads, preferred_element_type=jnp.float32
    ) * head_size ** (-0.5)
    top = jnp.max(scores, axis=-1, keepdims=True)
    weights = jnp.exp(scores - top)
    probs = (weights / jnp.sum(weights, axis=-1, keepdims=True)).astype(jnp.bfloat16)
    mixed = jnp.einsum("bhqk,bkhd->bqhd", probs, value_heads, preferred_element_type=jnp.float32)
    return mixed.reshape(batch, length, width).astype(jnp.bfloat16)


def add_rows(inputs, piece):
    return jnp.dot(inputs, piece, preferred_element_type=jnp.float32)


def body(
    clip,
    space_gain,
    space_qkv,
    space_out,
    mlp_gain,
    mlp_up,
    mlp_down,
    time_gain,
    time_qkv,
    time_out,
):
    clips, frames, patches, width = clip.shape
    rows = clip.reshape(-1, width)
    count = rows.shape[0]
    normed = layer_norm(rows, space_gain)
    packed = add_rows(normed, lax.all_gather(space_qkv, "fsdp", axis=0, tiled=True))
    packed = packed.astype(jnp.bfloat16).reshape(clips * frames, patches, 3 * width)
    query = packed[:, :, :width]
    keys = packed[:, :, width : 2 * width]
    values = packed[:, :, 2 * width :]
    keys_all, values_all = (
        lax.all_gather(keys, "fsdp", axis=1, tiled=True),
        lax.all_gather(values, "fsdp", axis=1, tiled=True),
    )
    space_att = heads_attend(query, keys_all, values_all).reshape(count, width)
    projected = add_rows(space_att, lax.all_gather(space_out, "fsdp", axis=0, tiled=True))
    first = (rows.astype(jnp.float32) + projected).astype(jnp.bfloat16)
    mlp_in = layer_norm(first, mlp_gain)
    inner = add_rows(mlp_in, lax.all_gather(mlp_up, "fsdp", axis=0, tiled=True))
    hidden = jax.nn.gelu(inner).astype(jnp.bfloat16)
    lowered = add_rows(hidden, lax.all_gather(mlp_down, "fsdp", axis=0, tiled=True))
    second = (first.astype(jnp.float32) + lowered).astype(jnp.bfloat16)
    grid = second.reshape(clips, frames, patches, width)
    moved = lax.all_to_all(grid, "dp", split_axis=2, concat_axis=1, tiled=True)
    all_frames = moved.shape[1]
    local_patches = moved.shape[2]
    series = moved.transpose(0, 2, 1, 3).reshape(-1, width)
    time_norm = layer_norm(series, time_gain)
    time_packed = add_rows(time_norm, lax.all_gather(time_qkv, "fsdp", axis=0, tiled=True))
    time_packed = time_packed.astype(jnp.bfloat16).reshape(
        clips * local_patches, all_frames, 3 * width
    )
    time_att = heads_attend(
        time_packed[:, :, :width],
        time_packed[:, :, width : 2 * width],
        time_packed[:, :, 2 * width :],
    )
    att_rows = time_att.reshape(count, width)
    done = (
        series.astype(jnp.float32)
        + add_rows(att_rows, lax.all_gather(time_out, "fsdp", axis=0, tiled=True))
    ).astype(jnp.bfloat16)
    done = done.reshape(clips, local_patches, all_frames, width).transpose(0, 2, 1, 3)
    encoded = lax.all_to_all(done, "dp", split_axis=1, concat_axis=2, tiled=True)
    return encoded


def solution(mesh):
    return jax.shard_map(
        body,
        mesh=mesh,
        in_specs=(
            P(None, "dp", "fsdp", None),
            P(),
            P("fsdp", None),
            P("fsdp", None),
            P(),
            P("fsdp", None),
            P("fsdp", None),
            P(),
            P("fsdp", None),
            P("fsdp", None),
        ),
        out_specs=P(None, "dp", "fsdp", None),
        check_vma=False,
    )
```

profile of v0, /device:TPU:1, one launch (start us, length us, event | category | flops | bytes accessed | tf_op | source)
XLA Modules:
  0.0 965.1 jit_solution(16846989617482358035)
XLA Ops:
  6.5 0.7 all-gather.9.cloned.1.call-update
  7.3 1.1 convert_reduce_fusion
  8.5 1.2 multiply_reduce_fusion.3
  9.7 1.2 fusion.28
  10.9 142.2 %all-gather.9.cloned.1.call-done = bf16[1024,3072]{1,0:T(8,128)(2,1)} async-done(((bf16[128,3072]{1,0:T(8,128)(2,1)}), bf16[1024,3072]{1,0:T(8,128)(2,1)}) %all-gather.9.cloned.1.call-update) | async-done | bytes 6291472 | tf_op jit(solution)/shard_map/all_gather | solution.py:53
  153.1 3.8 convolution_convert_fusion.1
  156.9 0.8 fusion.57
  157.8 0.7 all-gather.11.cloned.1.call-update
  158.6 0.5 all-gather.15.cloned.1.call-update
  159.1 0.5 all-gather.17.cloned.1.call-update
  159.7 0.5 all-gather.19.cloned.1.call-update
  160.3 0.7 all-gather.21.cloned.1.call-update
  161.1 0.7 all-gather.23.cloned.1.call-update
  161.8 0.3 reshape.161
  162.1 65.7 %all-gather.13.cloned.1.call-done = bf16[4,256,1024]{2,1,0:T(8,128)(2,1)} async-done(((bf16[4,32,1024]{2,1,0:T(8,128)(2,1)}), bf16[4,256,1024]{2,1,0:T(8,128)(2,1)}) %all-gather.13.cloned.1.call-update) | async-done | bytes 2097168 | tf_op jit(solution)/shard_map/all_gather | solution.py:59
  227.8 2.8 copy.48
  230.7 0.4 fusion.29
  231.1 1.3 copy-done.1
  232.5 0.7 fusion.58
  233.2 69.0 %all-gather.11.cloned.1.call-done = bf16[4,256,1024]{2,1,0:T(8,128)(2,1)} async-done(((bf16[4,32,1024]{2,1,0:T(8,128)(2,1)}), bf16[4,256,1024]{2,1,0:T(8,128)(2,1)}) %all-gather.11.cloned.1.call-update) | async-done | bytes 2097168 | tf_op jit(solution)/shard_map/all_gather | solution.py:60
  302.2 2.8 copy.47
  305.1 5.3 fusion.14
  310.3 0.2 copy.50
  310.6 0.3 convert_element_type.101
  310.9 65.5 %all-gather.15.cloned.1.call-done = bf16[1024,1024]{1,0:T(8,128)(2,1)} async-done(((bf16[128,1024]{1,0:T(8,128)(2,1)}), bf16[1024,1024]{1,0:T(8,128)(2,1)}) %all-gather.15.cloned.1.call-update) | async-done | bytes 2097168 | tf_op jit(solution)/shard_map/all_gather | solution.py:63
  376.4 2.1 fusion.59
  378.6 0.2 multiply_reduce_fusion.2
  378.8 169.9 %all-gather.17.cloned.1.call-done = bf16[1024,4096]{1,0:T(8,128)(2,1)} async-done(((bf16[128,4096]{1,0:T(8,128)(2,1)}), bf16[1024,4096]{1,0:T(8,128)(2,1)}) %all-gather.17.cloned.1.call-update) | async-done | bytes 8388624 | tf_op jit(solution)/shard_map/all_gather | solution.py:66
  548.7 170.5 %all-gather.19.cloned.1.call-done = bf16[4096,1024]{1,0:T(8,128)(2,1)} async-done(((bf16[512,1024]{1,0:T(8,128)(2,1)}), bf16[4096,1024]{1,0:T(8,128)(2,1)}) %all-gather.19.cloned.1.call-update) | async-done | bytes 8388624 | tf_op jit(solution)/shard_map/all_gather | solution.py:68
  719.2 8.5 fusion.15
  727.8 0.2 copy.51
  728.0 31.3 %all_to_all.27 = bf16[1,4,32,1024]{3,1,0,2:T(4,128)(2,1)S(1)} all-to-all(bf16[1,4,32,1024]{3,1,0,2:T(4,128)(2,1)S(1)} %copy.51), channel_id=1, replica_groups=mesh['dp'=32,'fsdp'=8] {'dp'}, dimensions={2} | all-to-all | bytes 524288 | tf_op jit(solution)/shard_map/all_to_all | solution.py:71
  759.6 0.3 multiply_reduce_fusion.1
  760.1 0.2 reshape.169
  760.3 100.1 %all-gather.21.cloned.1.call-done = bf16[1024,3072]{1,0:T(8,128)(2,1)} async-done(((bf16[128,3072]{1,0:T(8,128)(2,1)}), bf16[1024,3072]{1,0:T(8,128)(2,1)}) %all-gather.21.cloned.1.call-update) | async-done | bytes 6291472 | tf_op jit(solution)/shard_map/all_gather | solution.py:76
  860.4 3.8 fusion.2
  864.8 0.5 fusion.60
  865.3 0.4 convolution_multiply_fusion
  865.7 0.4 convolution_convert_fusion.3
  866.1 66.9 %all-gather.23.cloned.1.call-done = bf16[1024,1024]{1,0:T(8,128)(2,1)} async-done(((bf16[128,1024]{1,0:T(8,128)(2,1)}), bf16[1024,1024]{1,0:T(8,128)(2,1)}) %all-gather.23.cloned.1.call-update) | async-done | bytes 2097168 | tf_op jit(solution)/shard_map/all_gather | solution.py:88
  933.0 2.1 fusion.19
  935.1 0.4 copy.72
  935.5 0.5 broadcast.112
  936.0 2.1 reduce.10
  938.3 17.3 %all_to_all.28 = bf16[32,2,2048]{2,1,0:T(2,128)(2,1)S(1)} all-to-all(bf16[32,2,2048]{2,1,0:T(2,128)(2,1)S(1)} %reshape.173), channel_id=1, replica_groups=mesh['dp'=32,'fsdp'=8] {'dp'}, dimensions={0} | all-to-all | bytes 524288 | tf_op jit(solution)/shard_map/all_to_all | solution.py:91
  955.6 0.3 reshape.174
  955.9 1.5 bitcast_reduce_fusion
  957.5 0.8 copy.62
  (34 shorter events, 1.8 us)
Async XLA Ops:
  6.5 146.6 %all-gather.9.cloned.1.call-start = ((), (), s32[]{:S(2)}) async-start(), calls=%async_computation.2 | async-start | bytes 7077888 | tf_op jit(solution)/shard_map/all_gather | solution.py:53
  7.3 220.6 %all-gather.13.cloned.1.call-start = ((), (), s32[]{:S(2)}) async-start(), calls=%async_computation.4 | async-start | bytes 2359296 | tf_op jit(solution)/shard_map/all_gather | solution.py:59
  157.8 144.4 %all-gather.11.cloned.1.call-start = ((), (), s32[]{:S(2)}) async-start(), calls=%async_computation.3 | async-start | bytes 2359296 | tf_op jit(solution)/shard_map/all_gather | solution.py:60
  158.5 217.9 %all-gather.15.cloned.1.call-start = ((), (), s32[]{:S(2)}) async-start(), calls=%async_computation.5 | async-start | bytes 2359296 | tf_op jit(solution)/shard_map/all_gather | solution.py:63
  159.1 389.6 %all-gather.17.cloned.1.call-start = ((), (), s32[]{:S(2)}) async-start(), calls=%async_computation.6 | async-start | bytes 9437184 | tf_op jit(solution)/shard_map/all_gather | solution.py:66
  159.7 559.5 %all-gather.19.cloned.1.call-start = ((), (), s32[]{:S(2)}) async-start(), calls=%async_computation.7 | async-start | bytes 9437184 | tf_op jit(solution)/shard_map/all_gather | solution.py:68
  160.3 700.1 %all-gather.21.cloned.1.call-start = ((), (), s32[]{:S(2)}) async-start(), calls=%async_computation.8 | async-start | bytes 7077888 | tf_op jit(solution)/shard_map/all_gather | solution.py:76
  161.0 772.0 %all-gather.23.cloned.1.call-start = ((), (), s32[]{:S(2)}) async-start(), calls=%async_computation.9 | async-start | bytes 2359296 | tf_op jit(solution)/shard_map/all_gather | solution.py:88
  231.1 1.4 copy-start.1
  305.1 71.4 %copy-start = (bf16[1,4,32,1024]{3,2,1,0:T(8,128)(2,1)S(1)}, bf16[1,4,32,1024]{3,2,1,0:T(8,128)(2,1)}, u32[]{:S(2)}) copy-start(bf16[1,4,32,1024]{3,2,1,0:T(8,128)(2,1)} %param.10) | copy-start | bytes 786436
  310.6 408.7 %copy-start.3 = (f32[1024]{0:T(1024)S(1)}, f32[1024]{0:T(1024)}, u32[]{:S(2)}) copy-start(f32[1024]{0:T(1024)} %param.14) | copy-start | bytes 12292
  727.7 132.6 %copy-start.2 = (f32[1024]{0:T(1024)S(1)}, f32[1024]{0:T(1024)}, u32[]{:S(2)}) copy-start(f32[1024]{0:T(1024)} %param.17) | copy-start | bytes 12292
Sparse Core Ops, SparseCore 0:
  10.0 143.1 all-gather.8
  157.9 69.8 all-gather.12
  230.5 71.6 all-gather.10
  304.7 71.7 all-gather.14
  378.9 169.7 all-gather.16
  551.2 167.9 all-gather.18
  721.8 138.5 all-gather.20
  863.0 69.9 all-gather.22
where the time goes:
time: 966 us; the launch traced here: 965 us
  waiting for transfers between devices  854 us (88%)
  blocking collectives  48.6 us (5%)
  matrix products  27.2 us (3%)
  local copies, waits for them, and re-layouts  13.9 us (1%)
  between operations  13.8 us (1%)
    all_gather x1, waiting for transfers between devices, body(): lax.all_gather(mlp_down, 'fsdp', axis=0, tiled=True)  170 us
    all_gather x1, waiting for transfers between devices, body(): inner = add_rows(mlp_in, lax.all_gather(mlp_up, 'fsdp', axis=0, tiled=True))  170 us
    all_gather x1, waiting for transfers between devices, body(): lax.all_gather(space_qkv, 'fsdp', axis=0, tiled=True)  142 us
    all_gather x1, waiting for transfers between devices, body(): lax.all_gather(time_qkv, 'fsdp', axis=0, tiled=True)  100 us
    all_gather x1, waiting for transfers between devices, body(): lax.all_gather(values, 'fsdp', axis=1, tiled=True)  69 us
    all_gather x1, waiting for transfers between devices, body(): lax.all_gather(time_out, 'fsdp', axis=0, tiled=True)  66.9 us
    all_gather x1, waiting for transfers between devices, body(): lax.all_gather(keys, 'fsdp', axis=1, tiled=True)  65.7 us
    all_gather x1, waiting for transfers between devices, body(): lax.all_gather(space_out, 'fsdp', axis=0, tiled=True)  65.5 us
  transfers between devices with their start and end apart: 8, of which 8 were waited for; matrix products, arithmetic and copies ran while one was open for 4% of the time, Pallas kernels for 0%

commit v1 on v0

v1 whole, which is shorter than its diff:
```python
import functools

import jax
import jax.numpy as jnp
from jax import lax
from jax.experimental import pallas as pl
from jax.experimental.pallas import tpu as pltpu
from jax.sharding import PartitionSpec as P

BF = jnp.bfloat16
F32 = jnp.float32
AXES = ("dp", "fsdp")
PAIRS = 4
HALF = 512


def shift(v, x=0, y=0, z=0, c=0):
    pairs = []
    for sx in range(4):
        for sy in range(4):
            for sz in range(8):
                for sc in range(2):
                    tx, ty, tz, tc = (sx + x) % 4, (sy + y) % 4, (sz + z) % 8, (sc + c) % 2
                    here = (((sz % 4) * 4 + sy) * 2 + sc) * 8 + (sz // 4) * 4 + sx
                    there = (((tz % 4) * 4 + ty) * 2 + tc) * 8 + (tz // 4) * 4 + tx
                    pairs.append((here, there))
    return lax.ppermute(v, AXES, pairs)


def x_ring(near, far):
    rows = near.shape[0]
    both = jnp.concatenate([near, far], axis=0)
    from_left = shift(both, x=1)
    from_right = shift(both, x=-1)
    far_near = shift(from_left[:rows], x=1)
    far_far = shift(from_right[rows:], x=-1)
    return both, from_right, far_near, far_far, from_left


def y_ring(mine):
    rows = mine.shape[0] // 2
    from_below = shift(mine, y=1)
    from_above = shift(mine, y=-1)
    two_low = shift(from_below[:rows], y=1)
    two_high = shift(from_above[rows:], y=-1)
    return mine, from_above, two_low, two_high, from_below


def gather_group(alpha, beta_part):
    ra, rb = alpha.shape[0], beta_part.shape[0]
    near = jnp.concatenate([alpha, beta_part], axis=0)
    rows = ra + rb
    far = shift(near, z=4)
    both, right, two_near, two_far, left = x_ring(near, far)
    cut = lambda a, k: a[k * rows + ra : (k + 1) * rows]
    share = jnp.concatenate(
        [cut(both, 0), cut(right, 0), two_near[ra:], cut(left, 0),
         cut(both, 1), cut(right, 1), two_far[ra:], cut(left, 1)], axis=0)
    return (both, right, two_near, two_far, left), y_ring(share)


def norm_rows(wide, gain):
    centre = jnp.mean(wide, axis=-1, keepdims=True)
    off = wide - centre
    spread = jnp.mean(off * off, axis=-1, keepdims=True)
    return (off * lax.rsqrt(spread + 1e-06) * gain).astype(BF)


def x_pieces(refs, rows):
    both, right, two_near, two_far, left = refs
    return {
        (0, 0): (both, 0), (0, 1): (both, rows),
        (1, 0): (right, 0), (1, 1): (right, rows),
        (2, 0): (two_near, 0), (2, 1): (two_far, 0),
        (3, 0): (left, 0), (3, 1): (left, rows),
    }


def y_pieces(refs, rows):
    mine, above, two_low, two_high, below = refs
    found = {}
    for rz in range(2):
        for rx in range(4):
            at = (rz * 4 + rx) * rows
            found[0, rz, rx] = (mine, at)
            found[1, rz, rx] = (above, at)
            found[2, rz, rx] = (two_low, at) if rz == 0 else (two_high, at - 4 * rows)
            found[3, rz, rx] = (below, at)
    return found


def block_of(place, rx, rz):
    x, zh = place[0], place[1]
    return lax.rem(zh + rz, 2) * 4 + lax.rem(x + rx, 4)


def attend_kernel(seqs, place, tokens, gain, *refs):
    xs, ys = refs[:5], refs[5:10]
    out, wqkv, wout, packed, att, sems = refs[10:]
    copies = []

    def start(src, dst):
        copy = pltpu.make_async_copy(src, dst, sems.at[len(copies)])
        copy.start()
        copies.append(copy)

    for (ry, rz, rx), (ref, at) in y_pieces(ys, 64).items():
        y = lax.rem(place[2] + ry, 4)
        row = block_of(place, rx, rz) * 128 + lax.rem(y, 2) * 64
        column = lax.div(y, 2) * HALF
        start(ref.at[pl.ds(at, 64)],
              wqkv.at[pl.ds(pl.multiple_of(row, 64), 64), pl.ds(pl.multiple_of(column, HALF), HALF)])
    for (rx, rz), (ref, at) in x_pieces(xs, 320).items():
        block = block_of(place, rx, rz)
        start(ref.at[pl.ds(at, 128)],
              wqkv.at[pl.ds(pl.multiple_of(block * 128, 128), 128), pl.ds(2 * HALF, HALF)])
    need = len(copies)
    for (rx, rz), (ref, at) in x_pieces(xs, 320).items():
        row = pl.multiple_of(block_of(place, rx, rz) * 64, 64)
        for half in range(2):
            start(ref.at[pl.ds(at + 128 + half * 64, 64)],
                  wout.at[pl.ds(row, 64), pl.ds(half * HALF, HALF)])
    normed = norm_rows(tokens[...].astype(F32), gain[...])
    for copy in copies[:need]:
        copy.wait()
    for part in range(3):
        cols = slice(part * HALF, (part + 1) * HALF)
        got = jnp.dot(normed, wqkv[:, cols], preferred_element_type=F32)
        packed[:, cols] = got.astype(BF)
    length = tokens.shape[0] // seqs
    low = lax.broadcasted_iota(jnp.int32, (length, 128), 1) < 64
    for seq in range(seqs):
        rows = slice(seq * length, (seq + 1) * length)
        for pair in range(PAIRS):
            query = packed[rows, pair * 128 : pair * 128 + 128] * 0.125
            keys = packed[rows, HALF + pair * 128 : HALF + pair * 128 + 128]
            values = packed[rows, 2 * HALF + pair * 128 : 2 * HALF + pair * 128 + 128]
            mixed = []
            for mask in (low, jnp.logical_not(low)):
                one = jnp.where(mask, query, jnp.zeros_like(query))
                scores = lax.dot_general(one, keys, (((1,), (1,)), ((), ())), preferred_element_type=F32)
                weights = jnp.exp(scores - jnp.max(scores, axis=-1, keepdims=True))
                total = jnp.sum(weights, axis=-1, keepdims=True)
                probs = (weights / total).astype(BF)
                mixed.append(jnp.dot(probs, values, preferred_element_type=F32))
            att[rows, pair * 128 : pair * 128 + 128] = jnp.where(low, mixed[0], mixed[1]).astype(BF)
    for copy in copies[need:]:
        copy.wait()
    out[...] = jnp.dot(att[...], wout[...], preferred_element_type=F32)


def attend_call(seqs, place, tokens, gain, xs, ys):
    count, width = tokens.shape
    vmem = pl.BlockSpec(memory_space=pltpu.VMEM)
    return pl.pallas_call(
        functools.partial(attend_kernel, seqs),
        out_shape=jax.ShapeDtypeStruct((count, width), F32),
        in_specs=[pl.BlockSpec(memory_space=pltpu.SMEM), vmem, vmem] + [pl.BlockSpec(memory_space=pl.ANY)] * 10,
        out_specs=vmem,
        scratch_shapes=[
            pltpu.VMEM((width, 3 * HALF), BF),
            pltpu.VMEM((HALF, width), BF),
            pltpu.VMEM((count, 3 * HALF), BF),
            pltpu.VMEM((count, HALF), BF),
            pltpu.SemaphoreType.DMA((56,)),
        ],
        compiler_params=pltpu.CompilerParams(vmem_limit_bytes=32 * 1024 * 1024),
        cost_estimate=pl.CostEstimate(flops=1400000000, bytes_accessed=6000000, transcendentals=600000),
    )(place, tokens, gain, *xs, *ys)


def mlp_kernel(place, tokens, own, other, gain, *refs):
    xs, ys = refs[:5], refs[5:10]
    first, out, wup, wdown, hidden, sems = refs[10:]
    copies = []

    def start(src, dst):
        copy = pltpu.make_async_copy(src, dst, sems.at[len(copies)])
        copy.start()
        copies.append(copy)

    for (ry, rz, rx), (ref, at) in y_pieces(ys, 128).items():
        column = lax.rem(place[2] + ry, 4) * HALF
        row = block_of(place, rx, rz) * 128
        start(ref.at[pl.ds(at, 128)],
              wup.at[pl.ds(pl.multiple_of(row, 128), 128), pl.ds(pl.multiple_of(column, HALF), HALF)])
    need = len(copies)
    for (rx, rz), (ref, at) in x_pieces(xs, 640).items():
        row = pl.multiple_of(block_of(place, rx, rz) * 256, 256)
        for half in range(2):
            start(ref.at[pl.ds(at + half * 256, 256)],
                  wdown.at[pl.ds(row, 256), pl.ds(half * HALF, HALF)])
    summed = (tokens[...].astype(F32) + (own[...] + other[...])).astype(BF)
    first[...] = summed
    normed = norm_rows(summed.astype(F32), gain[...])
    for copy in copies[:need]:
        copy.wait()
    for part in range(4):
        cols = slice(part * HALF, (part + 1) * HALF)
        inner = jnp.dot(normed, wup[:, cols], preferred_element_type=F32)
        hidden[:, cols] = jax.nn.gelu(inner, approximate=True).astype(BF)
    for copy in copies[need:]:
        copy.wait()
    for part in range(2):
        cols = slice(part * HALF, (part + 1) * HALF)
        out[:, cols] = jnp.dot(hidden[...], wdown[:, cols], preferred_element_type=F32)


def mlp_call(place, tokens, own, other, gain, xs, ys):
    count, width = tokens.shape
    vmem = pl.BlockSpec(memory_space=pltpu.VMEM)
    return pl.pallas_call(
        mlp_kernel,
        out_shape=(jax.ShapeDtypeStruct((count, width), BF), jax.ShapeDtypeStruct((count, width), F32)),
        in_specs=[pl.BlockSpec(memory_space=pltpu.SMEM)] + [vmem] * 4 + [pl.BlockSpec(memory_space=pl.ANY)] * 10,
        out_specs=(vmem, vmem),
        scratch_shapes=[
            pltpu.VMEM((width, 4 * HALF), BF),
            pltpu.VMEM((4 * HALF, width), BF),
            pltpu.VMEM((count, 4 * HALF), BF),
            pltpu.SemaphoreType.DMA((48,)),
        ],
        compiler_params=pltpu.CompilerParams(vmem_limit_bytes=40 * 1024 * 1024),
        cost_estimate=pl.CostEstimate(flops=2200000000, bytes_accessed=11000000, transcendentals=600000),
    )(place, tokens, own, other, gain, *xs, *ys)


def core_half(c, a, b):
    return jnp.where(c == 0, a, b)


def attend_weights(c, y, qkv, project):
    rows, width = project.shape
    heads = qkv.reshape(rows, 3, 8, 2, 64)
    mine = core_half(c, heads[:, :, :, 0], heads[:, :, :, 1]).reshape(rows, 3, HALF)
    down = core_half(c, project[:64], project[64:])
    alpha = jnp.concatenate([mine[:, 2], down[:, :HALF], down[:, HALF:]], axis=0)
    beta = jnp.concatenate([mine[:, 0], mine[:, 1]], axis=0)
    return alpha, lax.dynamic_slice_in_dim(beta, y * 64, 64, axis=0)


def mlp_weights(c, y, up, down):
    mine = core_half(c, up.reshape(128, 8, 2, 256)[:, :, 0], up.reshape(128, 8, 2, 256)[:, :, 1]).reshape(128, 2048)
    part = lax.dynamic_slice_in_dim(mine, y * HALF, HALF, axis=1)
    low = core_half(c, down[:256], down[256:])
    return jnp.concatenate([low[:, :HALF], low[:, HALF:]], axis=0), part


def both_cores(c, v):
    other = shift(v, c=1)
    return core_half(c, jnp.concatenate([v, other], axis=0), jnp.concatenate([other, v], axis=0))


def body(clip, space_gain, space_qkv, space_out, mlp_gain, mlp_up, mlp_down, time_gain, time_qkv, time_out):
    dp, fs = lax.axis_index("dp"), lax.axis_index("fsdp")
    c, y = lax.rem(dp, 2), lax.rem(lax.div(dp, 2), 4)
    place = jnp.stack([lax.rem(fs, 4), lax.div(fs, 4), y]).astype(jnp.int32)
    width = clip.shape[-1]

    space = gather_group(*attend_weights(c, y, space_qkv, space_out))
    middle = gather_group(*mlp_weights(c, y, mlp_up, mlp_down))
    time = gather_group(*attend_weights(c, y, time_qkv, time_out))

    split = clip.reshape(4, 16, 2, width)
    keep = core_half(c, split[:, :, 0], split[:, :, 1])
    give = core_half(c, split[:, :, 1], split[:, :, 0])
    taken = shift(give, c=1)
    frames = core_half(c, jnp.concatenate([keep, taken], axis=0), jnp.concatenate([taken, keep], axis=0))
    frames = lax.all_to_all(frames, "fsdp", split_axis=0, concat_axis=0, tiled=True)
    frames = frames.transpose(1, 0, 2).reshape(128, width)
    tokens = both_cores(c, frames)

    partial = attend_call(1, place, tokens, space_gain.reshape(1, width), *space)
    first, lowered = mlp_call(place, tokens, partial, shift(partial, c=1), mlp_gain.reshape(1, width), *middle)
    mine = lax.dynamic_slice_in_dim(lowered, c * 128, 128, axis=0)
    away = lax.dynamic_slice_in_dim(lowered, (1 - c) * 128, 128, axis=0)
    kept = lax.dynamic_slice_in_dim(first, c * 128, 128, axis=0)
    second = (kept.astype(F32) + (mine + shift(away, c=1))).astype(BF)

    groups = [[(2 * m + core) * 8 + k for m in range(16) for k in range(8)] for core in range(2)]
    series = lax.all_to_all(second, AXES, split_axis=0, concat_axis=0, tiled=True, axis_index_groups=groups)
    partial = attend_call(2, place, both_cores(c, series), time_gain.reshape(1, width), *time)
    mine = lax.dynamic_slice_in_dim(partial, c * 128, 128, axis=0)
    away = lax.dynamic_slice_in_dim(partial, (1 - c) * 128, 128, axis=0)
    done = (series.astype(F32) + (mine + shift(away, c=1))).astype(BF)
    return lax.all_to_all(done.reshape(1, 128, 1, width), "dp", split_axis=1, concat_axis=2, tiled=True)


def solution(mesh):
    return jax.shard_map(
        body,
        mesh=mesh,
        in_specs=(
            P(None, "dp", "fsdp", None),
            P(),
            P("fsdp", None),
            P("fsdp", None),
            P(),
            P("fsdp", None),
            P("fsdp", None),
            P(),
            P("fsdp", None),
            P("fsdp", None),
        ),
        out_specs=P(None, "dp", "fsdp", None),
        check_vma=False,
    )
```

time: 966 us -> 303 us (0.31)
  waiting for transfers between devices: 854 us -> 81.3 us
  starting transfers between devices: 0.27 us -> 103 us
  local copies, waits for them, and re-layouts: 13.9 us -> 64.4 us
  blocking collectives: 48.6 us -> 18.1 us
  matrix products: 27.2 us -> 0 us
  Pallas kernels: 0 us -> 21.2 us
  between operations: 13.8 us -> 0.85 us
    all_gather x8 -> x0, waiting for transfers between devices: 850 us -> none  [the longest x1 170 us: body(): lax.all_gather(mlp_down, 'fsdp', axis=0, tiled=True)]
    ppermute x0 -> x33, starting transfers between devices: none -> 74.4 us  [shift(): return lax.ppermute(v, AXES, pairs)]
    ppermute x0 -> x33, waiting for transfers between devices: none -> 72.8 us  [shift(): return lax.ppermute(v, AXES, pairs)]
    unnamed x11 -> x110, local copies, waits for them, and re-layouts: 2.32 us -> 39.8 us
    all_to_all x2 -> x1, blocking collectives: 48.6 us -> 18.1 us  [body(): lax.all_to_all(done.reshape(1, 128, 1, width), 'dp', split_axis=1, concat...]
    all_to_all x0 -> x2, starting transfers between devices: none -> 28.6 us  [the longest x1 19.7 us: body(): lax.all_to_all(second, AXES, split_axis=0, concat_axis=0, tiled=True, axi...]
    dot_general x9 -> x0, matrix products: 26.7 us -> none  [the longest x5 20.3 us: add_rows(): return jnp.dot(inputs, piece, preferred_element_type=jnp.float32)]
    pallas_call x0 -> x3, Pallas kernels: none -> 21.2 us  [the longest x2 14.7 us: attend_call(): pl.pallas_call(functools.partial(attend_kernel, seqs), out_shape=jax.Shap...]
  transfers between devices with their start and end apart: 8 -> 35, of which waited for: 8 -> 12; matrix products, arithmetic and copies ran while one was open for 4% -> 17% of each run, Pallas kernels for 0% -> 4%
where the time goes in v1:
time: 303 us; the launch traced here: 298 us
  starting transfers between devices  103 us (34%)
  waiting for transfers between devices  81.3 us (27%)
  local copies, waits for them, and re-layouts  64.4 us (21%)
  Pallas kernels  21.2 us (7%)
  blocking collectives  18.1 us (6%)
  other arithmetic  8.85 us (3%)
    ppermute x33, starting transfers between devices, shift(): return lax.ppermute(v, AXES, pairs)  74.4 us
    ppermute x33, waiting for transfers between devices, shift(): return lax.ppermute(v, AXES, pairs)  72.8 us
    unnamed x110, local copies, waits for them, and re-layouts  39.8 us
    all_to_all x1, starting transfers between devices, body(): lax.all_to_all(second, AXES, split_axis=0, concat_axis=0, tiled=True, axi...  19.7 us
    all_to_all x1, blocking collectives, body(): lax.all_to_all(done.reshape(1, 128, 1, width), 'dp', split_axis=1, concat...  18.1 us
    pallas_call x2, Pallas kernels, attend_call(): pl.pallas_call(functools.partial(attend_kernel, seqs), out_shape=jax.Shap...  14.7 us
    all_to_all x1, starting transfers between devices, body(): lax.all_to_all(frames, 'fsdp', split_axis=0, concat_axis=0, tiled=True)  8.88 us
    all_to_all x1, waiting for transfers between devices, body(): lax.all_to_all(second, AXES, split_axis=0, concat_axis=0, tiled=True, axi...  8.47 us
  transfers between devices with their start and end apart: 35, of which 12 were waited for; matrix products, arithmetic and copies ran while one was open for 17% of the time, Pallas kernels for 4%

profile of v1, /device:TPU:1, one launch (start us, length us, event | category | flops | bytes accessed | tf_op | source)
XLA Modules:
  0.0 297.7 jit_solution(5441018403944529022)
XLA Ops:
  0.0 1.5 copy.54
  6.2 7.7 %collective-permute-start.2 = (bf16[320,512]{1,0:T(8,128)(2,1)}, bf16[320,512]{1,0:T(8,128)(2,1)S(1)}, u32[]{:S(2)}, u32[]{:S(2)}) collective-permute-start(bf16[320,512]{1,0:T(8,128)(2,1)} %pad_maximum_fusion.2), channel_id=1, source_target_pairs={{0,4},{8,12},{64,68},{72,76},{128,132},{136,140},{192,196},{200,20... | collective-permute-start | bytes 983048 | tf_op jit(solution)/shard_map/ppermute | solution.py:27
  14.7 1.5 fusion.8
  20.0 2.1 collective-permute-done.2
  23.5 1.8 collective-permute-start.4
  25.3 4.6 %collective-permute-start = (bf16[4,16,1024]{2,0,1:T(4,128)(2,1)S(1)}, bf16[4,16,1024]{2,0,1:T(4,128)(2,1)S(1)}, u32[]{:S(2)}, u32[]{:S(2)}) collective-permute-start(bf16[4,16,1024]{2,0,1:T(4,128)(2,1)S(1)} %fusion.2), channel_id=1, source_target_pairs={{0,8},{8,0},{64,72},{72,64},{128,136},{136,128},{192,200},{200,192... | collective-permute-start | bytes 393224 | tf_op jit(solution)/shard_map/ppermute | solution.py:27
  30.0 1.5 collective-permute-start.3
  32.8 8.9 %all-to-all-start = ((bf16[8,16,1024]{2,1,0:T(8,128)(2,1)}), bf16[8,16,1024]{2,1,0:T(8,128)(2,1)}, u32[]{:S(2)}, u32[]{:S(2)}) async-start(bf16[8,16,1024]{2,1,0:T(8,128)(2,1)} %copy.52), calls=%async_computation | async-start | bytes 524288 | tf_op jit(solution)/shard_map/all_to_all | solution.py:269
  41.7 1.5 collective-permute-start.5
  43.2 9.7 %collective-permute-done.12 = bf16[640,512]{1,0:T(8,128)(2,1)} collective-permute-done((bf16[640,512]{1,0:T(8,128)(2,1)S(1)}, bf16[640,512]{1,0:T(8,128)(2,1)}, u32[]{:S(2)}, u32[]{:S(2)}) %collective-permute-start.12) | collective-permute-done | bytes 655392 | tf_op jit(solution)/shard_map/ppermute | solution.py:27
  54.1 2.6 collective-permute-start.13
  57.7 2.8 collective-permute-start.6
  60.4 1.5 constant_dynamic-update-slice_fusion.11
  66.2 24.0 %collective-permute-done.6.refs_3_ = bf16[320,512]{1,0:T(8,128)(2,1)S(1)} collective-permute-done((bf16[320,512]{1,0:T(8,128)(2,1)S(1)}, bf16[320,512]{1,0:T(8,128)(2,1)S(1)}, u32[]{:S(2)}, u32[]{:S(2)}) %collective-permute-start.6) | collective-permute-done | bytes 327712 | tf_op jit(solution)/shard_map/ppermute | solution.py:27
  100.2 6.7 %collective-permute-start.1 = (bf16[128,1024]{1,0:T(8,128)(2,1)S(1)}, bf16[128,1024]{1,0:T(8,128)(2,1)}, u32[]{:S(2)}, u32[]{:S(2)}) collective-permute-start(bf16[128,1024]{1,0:T(8,128)(2,1)S(1)} %bitcast.76), channel_id=1, source_target_pairs={{0,8},{8,0},{64,72},{72,64},{128,136},{136,128},{192,200},{200,192... | collective-permute-start | bytes 786440 | tf_op jit(solution)/shard_map/ppermute | solution.py:27
  108.3 1.7 slice.256
  112.7 1.6 slice_dynamic-update-slice_fusion.5
  114.2 1.6 slice_dynamic-update-slice_fusion.4
  115.8 1.6 slice_dynamic-update-slice_fusion.3
  118.0 6.1 %collective-permute-done.16.refs_3_ = bf16[640,512]{1,0:T(8,128)(2,1)S(1)} collective-permute-done((bf16[640,512]{1,0:T(8,128)(2,1)S(1)}, bf16[640,512]{1,0:T(8,128)(2,1)S(1)}, u32[]{:S(2)}, u32[]{:S(2)}) %collective-permute-start.16) | collective-permute-done | bytes 655392 | tf_op jit(solution)/shard_map/ppermute | solution.py:27
  124.8 1.6 slice_dynamic-update-slice_fusion.refs_5_
  126.4 2.5 collective-permute-start.17
  131.0 2.7 collective-permute-start.10
  133.6 1.7 constant_dynamic-update-slice_fusion.14.refs_0_
  135.4 3.0 %collective-permute-start.25 = (bf16[640,512]{1,0:T(8,128)(2,1)}, bf16[640,512]{1,0:T(8,128)(2,1)}, u32[]{:S(2)}, u32[]{:S(2)}) collective-permute-start(bf16[640,512]{1,0:T(8,128)(2,1)} %constant_dynamic-update-slice_fusion.14.refs_0_), channel_id=1, source_target_pairs={{0,1},{8,9},{64,65},{72,73},{128,129},{136,137},{192,193},{200,201... | collective-permute-start | bytes 1966088 | tf_op jit(solution)/shard_map/ppermute | solution.py:27
  139.8 13.3 %collective-permute-done.10.refs_8_ = bf16[256,512]{1,0:T(8,128)(2,1)S(1)} collective-permute-done((bf16[256,512]{1,0:T(8,128)(2,1)S(1)}, bf16[256,512]{1,0:T(8,128)(2,1)S(1)}, u32[]{:S(2)}, u32[]{:S(2)}) %collective-permute-start.10) | collective-permute-done | bytes 262176 | tf_op jit(solution)/shard_map/ppermute | solution.py:27
  157.7 5.4 %shard_map.100.own = f32[256,1024]{1,0:T(8,128)S(1)} custom-call(s32[3]{0:T(128)S(1)} %pad_add_fusion.place, bf16[256,1024]{1,0:T(8,128)(2,1)S(1)} %maximum_select_fusion.tokens, f32[1,1024]{1,0:T(1,128)S(1)} %bitcast.61, bf16[640,512]{1,0:T(8,128)(2,1)} %constant_dynamic-update-slice_fusion.refs_0_, bf16[640,512]{1,0:T(8,128)(2,1)} %collective-permute-done.3.refs_1_, ...), custom_call_target="tpu_custom_call" | custom-call | flops 1400000000 | bytes 6000000 | tf_op jit(solution)/shard_map/pallas_call | solution.py:155
  163.1 5.0 %collective-permute-start.11 = (f32[256,1024]{1,0:T(8,128)S(1)}, f32[256,1024]{1,0:T(8,128)}, u32[]{:S(2)}, u32[]{:S(2)}) collective-permute-start(f32[256,1024]{1,0:T(8,128)S(1)} %shard_map.100.own), channel_id=1, source_target_pairs={{0,8},{8,0},{64,72},{72,64},{128,136},{136,128},{192,200},{200,192... | collective-permute-start | bytes 3145736 | tf_op jit(solution)/shard_map/ppermute | solution.py:27
  168.2 1.8 slice.280
  170.0 11.7 %collective-permute-start.26 = (bf16[320,512]{1,0:T(8,128)(2,1)}, bf16[320,512]{1,0:T(8,128)(2,1)}, u32[]{:S(2)}, u32[]{:S(2)}) collective-permute-start(bf16[320,512]{1,0:T(8,128)(2,1)} %slice.280), channel_id=1, source_target_pairs={{0,1},{8,9},{64,65},{72,73},{128,129},{136,137},{192,193},{200,201... | collective-permute-start | bytes 983048 | tf_op jit(solution)/shard_map/ppermute | solution.py:27
  185.9 2.8 collective-permute-start.20
  190.2 1.5 constant_dynamic-update-slice_fusion.24
  193.1 6.5 %collective-permute-done.19.refs_7_ = bf16[512,512]{1,0:T(8,128)(2,1)S(1)} collective-permute-done((bf16[512,512]{1,0:T(8,128)(2,1)S(1)}, bf16[512,512]{1,0:T(8,128)(2,1)S(1)}, u32[]{:S(2)}, u32[]{:S(2)}) %collective-permute-start.19) | collective-permute-done | bytes 524320 | tf_op jit(solution)/shard_map/ppermute | solution.py:27
  199.7 6.6 %shard_map.101 = (bf16[256,1024]{1,0:T(8,128)(2,1)S(1)}, f32[256,1024]{1,0:T(8,128)S(1)}) custom-call(s32[3]{0:T(128)S(1)} %pad_add_fusion.place, bf16[256,1024]{1,0:T(8,128)(2,1)S(1)} %maximum_select_fusion.tokens, f32[256,1024]{1,0:T(8,128)S(1)} %shard_map.100.own, f32[256,1024]{1,0:T(8,128)} %collective-permute-done.11.other, f32[1,1024]{1,0:T(1,128)S(1)} %bitcast.60, ...), custom_call_target="tpu_custom_call" | custom-call | flops 2200000000 | bytes 11000000 | tf_op jit(solution)/shard_map/pallas_call | solution.py:212
  207.6 1.5 constant_dynamic-update-slice_fusion.22
  214.2 19.7 %all-to-all-start.1 = ((bf16[128,2,512]{2,1,0:T(2,128)(2,1)}), bf16[128,2,512]{2,1,0:T(2,128)(2,1)S(1)}, u32[]{:S(2)}, u32[]{:S(2)}) async-start(bf16[128,2,512]{2,1,0:T(2,128)(2,1)} %reshape.59), calls=%async_computation.1 | async-start | bytes 524288 | tf_op jit(solution)/shard_map/all_to_all | solution.py:281
  235.9 2.1 collective-permute-start.28
  238.0 8.5 %all-to-all-done.1 = bf16[128,2,512]{2,1,0:T(2,128)(2,1)S(1)} async-done(((bf16[128,2,512]{2,1,0:T(2,128)(2,1)}), bf16[128,2,512]{2,1,0:T(2,128)(2,1)S(1)}, u32[]{:S(2)}, u32[]{:S(2)}) %all-to-all-start.1) | async-done | bytes 262176 | tf_op jit(solution)/shard_map/all_to_all | solution.py:281
  246.8 2.2 collective-permute-start.22
  249.0 3.6 %collective-permute-done.29.refs_9_ = bf16[512,512]{1,0:T(8,128)(2,1)S(1)} collective-permute-done((bf16[512,512]{1,0:T(8,128)(2,1)}, bf16[512,512]{1,0:T(8,128)(2,1)S(1)}, u32[]{:S(2)}, u32[]{:S(2)}) %collective-permute-start.29) | collective-permute-done | bytes 524320 | tf_op jit(solution)/shard_map/ppermute | solution.py:27
  253.0 2.7 collective-permute-start.31
  255.9 5.2 %collective-permute-done.30.refs_7_ = bf16[256,512]{1,0:T(8,128)(2,1)S(1)} collective-permute-done((bf16[256,512]{1,0:T(8,128)(2,1)S(1)}, bf16[256,512]{1,0:T(8,128)(2,1)S(1)}, u32[]{:S(2)}, u32[]{:S(2)}) %collective-permute-start.30) | collective-permute-done | bytes 262176 | tf_op jit(solution)/shard_map/ppermute | solution.py:27
  261.1 9.2 %shard_map.102 = f32[256,1024]{1,0:T(8,128)S(1)} custom-call(s32[3]{0:T(128)S(1)} %pad_add_fusion.place, bf16[256,1024]{1,0:T(8,128)(2,1)S(1)} %maximum_select_fusion.1.tokens, f32[1,1024]{1,0:T(1,128)S(1)} %bitcast.62, bf16[640,512]{1,0:T(8,128)(2,1)} %constant_dynamic-update-slice_fusion.14.refs_0_, bf16[640,512]{1,0:T(8,128)(2,1)} %collective-permute-done.24.refs_1_, ...), custom_call_target="tpu_custom_call" | custom-call | flops 1400000000 | bytes 6000000 | tf_op jit(solution)/shard_map/pallas_call | solution.py:155
  270.4 1.9 collective-permute-start.32
  272.3 1.5 collective-permute-done.32
  274.4 2.1 reduce.3
  276.7 18.1 %all_to_all.35 = bf16[32,2,2048]{2,1,0:T(2,128)(2,1)S(1)} all-to-all(bf16[32,2,2048]{2,1,0:T(2,128)(2,1)S(1)} %reshape.61), channel_id=1, replica_groups=mesh['dp'=32,'fsdp'=8] {'dp'}, dimensions={0} | all-to-all | bytes 524288 | tf_op jit(solution)/shard_map/all_to_all | solution.py:286
  295.1 1.5 bitcast_reduce_fusion
  (190 shorter events, 60.2 us)
Async XLA Ops:
  6.2 15.8 %collective-permute-start.2 = (bf16[320,512]{1,0:T(8,128)(2,1)}, bf16[320,512]{1,0:T(8,128)(2,1)S(1)}, u32[]{:S(2)}, u32[]{:S(2)}) collective-permute-start(bf16[320,512]{1,0:T(8,128)(2,1)} %pad_maximum_fusion.2), channel_id=1, source_target_pairs={{0,4},{8,12},{64,68},{72,76},{128,132},{136,140},{192,196},{200,20... | collective-permute-start | bytes 983048 | tf_op jit(solution)/shard_map/ppermute | solution.py:27
  18.3 34.6 %collective-permute-start.12 = (bf16[640,512]{1,0:T(8,128)(2,1)S(1)}, bf16[640,512]{1,0:T(8,128)(2,1)}, u32[]{:S(2)}, u32[]{:S(2)}) collective-permute-start(bf16[640,512]{1,0:T(8,128)(2,1)S(1)} %pad_maximum_fusion.1), channel_id=1, source_target_pairs={{0,4},{8,12},{64,68},{72,76},{128,132},{136,140},{192,196},{200,20... | collective-permute-start | bytes 1966088 | tf_op jit(solution)/shard_map/ppermute | solution.py:27
  23.5 18.2 %collective-permute-start.4 = (bf16[640,512]{1,0:T(8,128)(2,1)}, bf16[640,512]{1,0:T(8,128)(2,1)S(1)}, u32[]{:S(2)}, u32[]{:S(2)}) collective-permute-start(bf16[640,512]{1,0:T(8,128)(2,1)} %constant_dynamic-update-slice_fusion.refs_0_), channel_id=1, source_target_pairs={{0,1},{8,9},{64,65},{72,73},{128,129},{136,137},{192,193},{200,201... | collective-permute-start | bytes 1966088 | tf_op jit(solution)/shard_map/ppermute | solution.py:27
  25.3 6.4 %collective-permute-start = (bf16[4,16,1024]{2,0,1:T(4,128)(2,1)S(1)}, bf16[4,16,1024]{2,0,1:T(4,128)(2,1)S(1)}, u32[]{:S(2)}, u32[]{:S(2)}) collective-permute-start(bf16[4,16,1024]{2,0,1:T(4,128)(2,1)S(1)} %fusion.2), channel_id=1, source_target_pairs={{0,8},{8,0},{64,72},{72,64},{128,136},{136,128},{192,200},{200,192... | collective-permute-start | bytes 393224 | tf_op jit(solution)/shard_map/ppermute | solution.py:27
  30.0 26.7 %collective-permute-start.3 = (bf16[640,512]{1,0:T(8,128)(2,1)}, bf16[640,512]{1,0:T(8,128)(2,1)}, u32[]{:S(2)}, u32[]{:S(2)}) collective-permute-start(bf16[640,512]{1,0:T(8,128)(2,1)} %constant_dynamic-update-slice_fusion.refs_0_), channel_id=1, source_target_pairs={{0,3},{8,11},{64,67},{72,75},{128,131},{136,139},{192,195},{200,20... | collective-permute-start | bytes 1966088 | tf_op jit(solution)/shard_map/ppermute | solution.py:27
  31.7 65.6 %copy-start.25 = (bf16[64,1024]{1,0:T(8,128)(2,1)}, bf16[64,1024]{1,0:T(8,128)(2,1)S(1)}, u32[]{:S(2)}) copy-start(bf16[64,1024]{1,0:T(8,128)(2,1)S(1)} %slice_select_fusion.3) | copy-start | bytes 393220
  32.8 66.3 %all-to-all-start = ((bf16[8,16,1024]{2,1,0:T(8,128)(2,1)}), bf16[8,16,1024]{2,1,0:T(8,128)(2,1)}, u32[]{:S(2)}, u32[]{:S(2)}) async-start(bf16[8,16,1024]{2,1,0:T(8,128)(2,1)} %copy.52), calls=%async_computation | async-start | bytes 524288 | tf_op jit(solution)/shard_map/all_to_all | solution.py:269
  41.7 20.2 %collective-permute-start.5 = (bf16[320,512]{1,0:T(8,128)(2,1)S(1)}, bf16[320,512]{1,0:T(8,128)(2,1)S(1)}, u32[]{:S(2)}, u32[]{:S(2)}) collective-permute-start(bf16[320,512]{1,0:T(8,128)(2,1)S(1)} %slice.247), channel_id=1, source_target_pairs={{0,1},{8,9},{64,65},{72,73},{128,129},{136,137},{192,193},{200,201... | collective-permute-start | bytes 983048 | tf_op jit(solution)/shard_map/ppermute | solution.py:27
  54.1 55.9 %collective-permute-start.13 = (bf16[1280,512]{1,0:T(8,128)(2,1)S(1)}, bf16[1280,512]{1,0:T(8,128)(2,1)S(1)}, u32[]{:S(2)}, u32[]{:S(2)}) collective-permute-start(bf16[1280,512]{1,0:T(8,128)(2,1)S(1)} %pad_maximum_fusion.refs_0_), channel_id=1, source_target_pairs={{0,3},{8,11},{64,67},{72,75},{128,131},{136,139},{192,195},{200,20... | collective-permute-start | bytes 3932168 | tf_op jit(solution)/shard_map/ppermute | solution.py:27
  56.7 36.8 %collective-permute-start.14 = (bf16[1280,512]{1,0:T(8,128)(2,1)S(1)}, bf16[1280,512]{1,0:T(8,128)(2,1)S(1)}, u32[]{:S(2)}, u32[]{:S(2)}) collective-permute-start(bf16[1280,512]{1,0:T(8,128)(2,1)S(1)} %pad_maximum_fusion.refs_0_), channel_id=1, source_target_pairs={{0,1},{8,9},{64,65},{72,73},{128,129},{136,137},{192,193},{200,201... | collective-permute-start | bytes 3932168 | tf_op jit(solution)/shard_map/ppermute | solution.py:27
  57.7 32.5 %collective-permute-start.6 = (bf16[320,512]{1,0:T(8,128)(2,1)S(1)}, bf16[320,512]{1,0:T(8,128)(2,1)S(1)}, u32[]{:S(2)}, u32[]{:S(2)}) collective-permute-start(bf16[320,512]{1,0:T(8,128)(2,1)S(1)} %slice.248), channel_id=1, source_target_pairs={{0,3},{8,11},{64,67},{72,75},{128,131},{136,139},{192,195},{200,20... | collective-permute-start | bytes 983048 | tf_op jit(solution)/shard_map/ppermute | solution.py:27
  61.9 36.0 %copy-start.8 = (bf16[320,512]{1,0:T(8,128)(2,1)}, bf16[320,512]{1,0:T(8,128)(2,1)S(1)}, u32[]{:S(2)}) copy-start(bf16[320,512]{1,0:T(8,128)(2,1)S(1)} %collective-permute-done.5.refs_2_) | copy-start | bytes 983044
  62.6 35.3 %copy-start.28 = (bf16[64,512]{1,0:T(8,128)(2,1)S(1)}, bf16[64,512]{1,0:T(8,128)(2,1)}, u32[]{:S(2)}) copy-start(bf16[64,512]{1,0:T(8,128)(2,1)} %get-tuple-element.32) | copy-start | bytes 196612
  92.2 14.8 %collective-permute-start.8 = (bf16[512,512]{1,0:T(8,128)(2,1)}, bf16[512,512]{1,0:T(8,128)(2,1)}, u32[]{:S(2)}, u32[]{:S(2)}) collective-permute-start(bf16[512,512]{1,0:T(8,128)(2,1)} %constant_dynamic-update-slice_fusion.5.refs_5_), channel_id=1, source_target_pairs={{0,16},{8,24},{64,80},{72,88},{128,144},{136,152},{192,208},{200,2... | collective-permute-start | bytes 1572872 | tf_op jit(solution)/shard_map/ppermute | solution.py:27
  95.5 16.0 %collective-permute-start.15 = (bf16[640,512]{1,0:T(8,128)(2,1)}, bf16[640,512]{1,0:T(8,128)(2,1)}, u32[]{:S(2)}, u32[]{:S(2)}) collective-permute-start(bf16[640,512]{1,0:T(8,128)(2,1)} %slice.262), channel_id=1, source_target_pairs={{0,1},{8,9},{64,65},{72,73},{128,129},{136,137},{192,193},{200,201... | collective-permute-start | bytes 1966088 | tf_op jit(solution)/shard_map/ppermute | solution.py:27
  98.6 32.3 %collective-permute-start.23 = (bf16[320,512]{1,0:T(8,128)(2,1)}, bf16[320,512]{1,0:T(8,128)(2,1)}, u32[]{:S(2)}, u32[]{:S(2)}) collective-permute-start(bf16[320,512]{1,0:T(8,128)(2,1)} %pad_maximum_fusion.3), channel_id=1, source_target_pairs={{0,4},{8,12},{64,68},{72,76},{128,132},{136,140},{192,196},{200,20... | collective-permute-start | bytes 983048 | tf_op jit(solution)/shard_map/ppermute | solution.py:27
  100.2 15.6 %copy-start.23 = (bf16[16,8,1024]{2,1,0:T(8,128)(2,1)}, bf16[16,8,1024]{2,1,0:T(8,128)(2,1)S(1)}, u32[]{:S(2)}) copy-start(bf16[16,8,1024]{2,1,0:T(8,128)(2,1)S(1)} %copy.87) | copy-start | bytes 786436
  100.2 35.1 %collective-permute-start.1 = (bf16[128,1024]{1,0:T(8,128)(2,1)S(1)}, bf16[128,1024]{1,0:T(8,128)(2,1)}, u32[]{:S(2)}, u32[]{:S(2)}) collective-permute-start(bf16[128,1024]{1,0:T(8,128)(2,1)S(1)} %bitcast.76), channel_id=1, source_target_pairs={{0,8},{8,0},{64,72},{72,64},{128,136},{136,128},{192,200},{200,192... | collective-permute-start | bytes 786440 | tf_op jit(solution)/shard_map/ppermute | solution.py:27
  106.9 21.9 %collective-permute-start.7 = (bf16[512,512]{1,0:T(8,128)(2,1)}, bf16[512,512]{1,0:T(8,128)(2,1)S(1)}, u32[]{:S(2)}, u32[]{:S(2)}) collective-permute-start(bf16[512,512]{1,0:T(8,128)(2,1)} %constant_dynamic-update-slice_fusion.5.refs_5_), channel_id=1, source_target_pairs={{0,48},{8,56},{64,112},{72,120},{128,176},{136,184},{192,240},{200... | collective-permute-start | bytes 1572872 | tf_op jit(solution)/shard_map/ppermute | solution.py:27
  110.0 18.9 %copy-start.26 = (bf16[64,1024]{1,0:T(8,128)(2,1)S(1)}, bf16[64,1024]{1,0:T(8,128)(2,1)}, u32[]{:S(2)}) copy-start(bf16[64,1024]{1,0:T(8,128)(2,1)} %copy-done.25) | copy-start | bytes 393220
  110.0 28.4 %collective-permute-start.9 = (bf16[256,512]{1,0:T(8,128)(2,1)}, bf16[256,512]{1,0:T(8,128)(2,1)S(1)}, u32[]{:S(2)}, u32[]{:S(2)}) collective-permute-start(bf16[256,512]{1,0:T(8,128)(2,1)} %slice.256), channel_id=1, source_target_pairs={{0,16},{8,24},{64,80},{72,88},{128,144},{136,152},{192,208},{200,2... | collective-permute-start | bytes 786440 | tf_op jit(solution)/shard_map/ppermute | solution.py:27
  110.2 19.3 %copy-start.29 = (bf16[64,512]{1,0:T(8,128)(2,1)S(1)}, bf16[64,512]{1,0:T(8,128)(2,1)}, u32[]{:S(2)}) copy-start(bf16[64,512]{1,0:T(8,128)(2,1)} %get-tuple-element.32) | copy-start | bytes 196612
  111.5 12.6 %collective-permute-start.16 = (bf16[640,512]{1,0:T(8,128)(2,1)S(1)}, bf16[640,512]{1,0:T(8,128)(2,1)S(1)}, u32[]{:S(2)}, u32[]{:S(2)}) collective-permute-start(bf16[640,512]{1,0:T(8,128)(2,1)S(1)} %slice.263), channel_id=1, source_target_pairs={{0,3},{8,11},{64,67},{72,75},{128,131},{136,139},{192,195},{200,20... | collective-permute-start | bytes 1966088 | tf_op jit(solution)/shard_map/ppermute | solution.py:27
  126.4 27.5 %copy-start.19 = (f32[1024]{0:T(1024)S(1)}, f32[1024]{0:T(1024)}, u32[]{:S(2)}) copy-start(f32[1024]{0:T(1024)} %param.11) | copy-start | bytes 12292
  126.4 58.4 %collective-permute-start.17 = (bf16[1024,512]{1,0:T(8,128)(2,1)}, bf16[1024,512]{1,0:T(8,128)(2,1)}, u32[]{:S(2)}, u32[]{:S(2)}) collective-permute-start(bf16[1024,512]{1,0:T(8,128)(2,1)} %slice_dynamic-update-slice_fusion.refs_5_), channel_id=1, source_target_pairs={{0,48},{8,56},{64,112},{72,120},{128,176},{136,184},{192,240},{200... | collective-permute-start | bytes 3145736 | tf_op jit(solution)/shard_map/ppermute | solution.py:27
  128.9 54.0 %collective-permute-start.18 = (bf16[1024,512]{1,0:T(8,128)(2,1)}, bf16[1024,512]{1,0:T(8,128)(2,1)}, u32[]{:S(2)}, u32[]{:S(2)}) collective-permute-start(bf16[1024,512]{1,0:T(8,128)(2,1)} %slice_dynamic-update-slice_fusion.refs_5_), channel_id=1, source_target_pairs={{0,16},{8,24},{64,80},{72,88},{128,144},{136,152},{192,208},{200,2... | collective-permute-start | bytes 3145736 | tf_op jit(solution)/shard_map/ppermute | solution.py:27
  131.0 22.2 %collective-permute-start.10 = (bf16[256,512]{1,0:T(8,128)(2,1)S(1)}, bf16[256,512]{1,0:T(8,128)(2,1)S(1)}, u32[]{:S(2)}, u32[]{:S(2)}) collective-permute-start(bf16[256,512]{1,0:T(8,128)(2,1)S(1)} %slice.257), channel_id=1, source_target_pairs={{0,48},{8,56},{64,112},{72,120},{128,176},{136,184},{192,240},{200... | collective-permute-start | bytes 786440 | tf_op jit(solution)/shard_map/ppermute | solution.py:27
  135.4 32.8 %collective-permute-start.25 = (bf16[640,512]{1,0:T(8,128)(2,1)}, bf16[640,512]{1,0:T(8,128)(2,1)}, u32[]{:S(2)}, u32[]{:S(2)}) collective-permute-start(bf16[640,512]{1,0:T(8,128)(2,1)} %constant_dynamic-update-slice_fusion.14.refs_0_), channel_id=1, source_target_pairs={{0,1},{8,9},{64,65},{72,73},{128,129},{136,137},{192,193},{200,201... | collective-permute-start | bytes 1966088 | tf_op jit(solution)/shard_map/ppermute | solution.py:27
  138.4 15.5 %copy-start.5 = (bf16[512,512]{1,0:T(8,128)(2,1)S(1)}, bf16[512,512]{1,0:T(8,128)(2,1)}, u32[]{:S(2)}) copy-start(bf16[512,512]{1,0:T(8,128)(2,1)} %copy-done.4) | copy-start | bytes 1572868
  138.4 14.8 %copy-start.14 = (bf16[256,512]{1,0:T(8,128)(2,1)}, bf16[256,512]{1,0:T(8,128)(2,1)S(1)}, u32[]{:S(2)}) copy-start(bf16[256,512]{1,0:T(8,128)(2,1)S(1)} %collective-permute-done.9.refs_7_) | copy-start | bytes 786436
  138.4 43.3 %collective-permute-start.24 = (bf16[640,512]{1,0:T(8,128)(2,1)}, bf16[640,512]{1,0:T(8,128)(2,1)}, u32[]{:S(2)}, u32[]{:S(2)}) collective-permute-start(bf16[640,512]{1,0:T(8,128)(2,1)} %constant_dynamic-update-slice_fusion.14.refs_0_), channel_id=1, source_target_pairs={{0,3},{8,11},{64,67},{72,75},{128,131},{136,139},{192,195},{200,20... | collective-permute-start | bytes 1966088 | tf_op jit(solution)/shard_map/ppermute | solution.py:27
  163.1 30.0 %collective-permute-start.11 = (f32[256,1024]{1,0:T(8,128)S(1)}, f32[256,1024]{1,0:T(8,128)}, u32[]{:S(2)}, u32[]{:S(2)}) collective-permute-start(f32[256,1024]{1,0:T(8,128)S(1)} %shard_map.100.own), channel_id=1, source_target_pairs={{0,8},{8,0},{64,72},{72,64},{128,136},{136,128},{192,200},{200,192... | collective-permute-start | bytes 3145736 | tf_op jit(solution)/shard_map/ppermute | solution.py:27
  168.2 31.5 %copy-start.7 = (bf16[640,512]{1,0:T(8,128)(2,1)S(1)}, bf16[640,512]{1,0:T(8,128)(2,1)}, u32[]{:S(2)}) copy-start(bf16[640,512]{1,0:T(8,128)(2,1)} %copy-done.6) | copy-start | bytes 1966084
  170.0 20.2 %collective-permute-start.26 = (bf16[320,512]{1,0:T(8,128)(2,1)}, bf16[320,512]{1,0:T(8,128)(2,1)}, u32[]{:S(2)}, u32[]{:S(2)}) collective-permute-start(bf16[320,512]{1,0:T(8,128)(2,1)} %slice.280), channel_id=1, source_target_pairs={{0,1},{8,9},{64,65},{72,73},{128,129},{136,137},{192,193},{200,201... | collective-permute-start | bytes 983048 | tf_op jit(solution)/shard_map/ppermute | solution.py:27
  181.6 18.1 %copy-start.3 = (bf16[1280,512]{1,0:T(8,128)(2,1)S(1)}, bf16[1280,512]{1,0:T(8,128)(2,1)}, u32[]{:S(2)}) copy-start(bf16[1280,512]{1,0:T(8,128)(2,1)} %copy-done.2) | copy-start | bytes 3932164
  182.7 17.0 %copy-start.1 = (bf16[1280,512]{1,0:T(8,128)(2,1)S(1)}, bf16[1280,512]{1,0:T(8,128)(2,1)}, u32[]{:S(2)}) copy-start(bf16[1280,512]{1,0:T(8,128)(2,1)} %copy-done) | copy-start | bytes 3932164
  182.7 17.0 %copy-start.18 = (f32[1024]{0:T(1024)S(1)}, f32[1024]{0:T(1024)}, u32[]{:S(2)}) copy-start(f32[1024]{0:T(1024)} %param.14) | copy-start | bytes 12292
  182.8 27.8 %collective-permute-start.27 = (bf16[320,512]{1,0:T(8,128)(2,1)S(1)}, bf16[320,512]{1,0:T(8,128)(2,1)S(1)}, u32[]{:S(2)}, u32[]{:S(2)}) collective-permute-start(bf16[320,512]{1,0:T(8,128)(2,1)S(1)} %slice.281), channel_id=1, source_target_pairs={{0,3},{8,11},{64,67},{72,75},{128,131},{136,139},{192,195},{200,20... | collective-permute-start | bytes 983048 | tf_op jit(solution)/shard_map/ppermute | solution.py:27
  184.0 15.6 %collective-permute-start.19 = (bf16[512,512]{1,0:T(8,128)(2,1)S(1)}, bf16[512,512]{1,0:T(8,128)(2,1)S(1)}, u32[]{:S(2)}, u32[]{:S(2)}) collective-permute-start(bf16[512,512]{1,0:T(8,128)(2,1)S(1)} %slice.271), channel_id=1, source_target_pairs={{0,16},{8,24},{64,80},{72,88},{128,144},{136,152},{192,208},{200,2... | collective-permute-start | bytes 1572872 | tf_op jit(solution)/shard_map/ppermute | solution.py:27
  185.9 13.8 %collective-permute-start.20 = (bf16[512,512]{1,0:T(8,128)(2,1)S(1)}, bf16[512,512]{1,0:T(8,128)(2,1)S(1)}, u32[]{:S(2)}, u32[]{:S(2)}) collective-permute-start(bf16[512,512]{1,0:T(8,128)(2,1)S(1)} %slice.272), channel_id=1, source_target_pairs={{0,48},{8,56},{64,112},{72,120},{128,176},{136,184},{192,240},{200... | collective-permute-start | bytes 1572872 | tf_op jit(solution)/shard_map/ppermute | solution.py:27
  206.4 5.5 %collective-permute-start.21 = (f32[128,1024]{1,0:T(8,128)S(1)}, f32[128,1024]{1,0:T(8,128)S(1)}, u32[]{:S(2)}, u32[]{:S(2)}) collective-permute-start(f32[128,1024]{1,0:T(8,128)S(1)} %constant_dynamic-slice_fusion.1), channel_id=1, source_target_pairs={{0,8},{8,0},{64,72},{72,64},{128,136},{136,128},{192,200},{200,192... | collective-permute-start | bytes 1572872 | tf_op jit(solution)/shard_map/ppermute | solution.py:27
  214.2 32.3 %all-to-all-start.1 = ((bf16[128,2,512]{2,1,0:T(2,128)(2,1)}), bf16[128,2,512]{2,1,0:T(2,128)(2,1)S(1)}, u32[]{:S(2)}, u32[]{:S(2)}) async-start(bf16[128,2,512]{2,1,0:T(2,128)(2,1)} %reshape.59), calls=%async_computation.1 | async-start | bytes 524288 | tf_op jit(solution)/shard_map/all_to_all | solution.py:281
  235.3 17.3 %collective-permute-start.29 = (bf16[512,512]{1,0:T(8,128)(2,1)}, bf16[512,512]{1,0:T(8,128)(2,1)S(1)}, u32[]{:S(2)}, u32[]{:S(2)}) collective-permute-start(bf16[512,512]{1,0:T(8,128)(2,1)} %constant_dynamic-update-slice_fusion.19.refs_5_), channel_id=1, source_target_pairs={{0,16},{8,24},{64,80},{72,88},{128,144},{136,152},{192,208},{200,2... | collective-permute-start | bytes 1572872 | tf_op jit(solution)/shard_map/ppermute | solution.py:27
  235.9 17.1 %collective-permute-start.28 = (bf16[512,512]{1,0:T(8,128)(2,1)}, bf16[512,512]{1,0:T(8,128)(2,1)S(1)}, u32[]{:S(2)}, u32[]{:S(2)}) collective-permute-start(bf16[512,512]{1,0:T(8,128)(2,1)} %constant_dynamic-update-slice_fusion.19.refs_5_), channel_id=1, source_target_pairs={{0,48},{8,56},{64,112},{72,120},{128,176},{136,184},{192,240},{200... | collective-permute-start | bytes 1572872 | tf_op jit(solution)/shard_map/ppermute | solution.py:27
  246.8 9.0 %collective-permute-start.22 = (bf16[128,1024]{1,0:T(8,128)(2,1)S(1)}, bf16[128,1024]{1,0:T(8,128)(2,1)S(1)}, u32[]{:S(2)}, u32[]{:S(2)}) collective-permute-start(bf16[128,1024]{1,0:T(8,128)(2,1)S(1)} %bitcast.73), channel_id=1, source_target_pairs={{0,8},{8,0},{64,72},{72,64},{128,136},{136,128},{192,200},{200,192... | collective-permute-start | bytes 786440 | tf_op jit(solution)/shard_map/ppermute | solution.py:27
  252.7 8.4 %collective-permute-start.30 = (bf16[256,512]{1,0:T(8,128)(2,1)S(1)}, bf16[256,512]{1,0:T(8,128)(2,1)S(1)}, u32[]{:S(2)}, u32[]{:S(2)}) collective-permute-start(bf16[256,512]{1,0:T(8,128)(2,1)S(1)} %slice.289), channel_id=1, source_target_pairs={{0,16},{8,24},{64,80},{72,88},{128,144},{136,152},{192,208},{200,2... | collective-permute-start | bytes 786440 | tf_op jit(solution)/shard_map/ppermute | solution.py:27
  253.0 8.1 %collective-permute-start.31 = (bf16[256,512]{1,0:T(8,128)(2,1)S(1)}, bf16[256,512]{1,0:T(8,128)(2,1)S(1)}, u32[]{:S(2)}, u32[]{:S(2)}) collective-permute-start(bf16[256,512]{1,0:T(8,128)(2,1)S(1)} %slice.290), channel_id=1, source_target_pairs={{0,48},{8,56},{64,112},{72,120},{128,176},{136,184},{192,240},{200... | collective-permute-start | bytes 786440 | tf_op jit(solution)/shard_map/ppermute | solution.py:27
  270.4 3.4 %collective-permute-start.32 = (f32[128,1024]{1,0:T(8,128)S(1)}, f32[128,1024]{1,0:T(8,128)S(1)}, u32[]{:S(2)}, u32[]{:S(2)}) collective-permute-start(f32[128,1024]{1,0:T(8,128)S(1)} %constant_dynamic-slice_fusion), channel_id=1, source_target_pairs={{0,8},{8,0},{64,72},{72,64},{128,136},{136,128},{192,200},{200,192... | collective-permute-start | bytes 1572872 | tf_op jit(solution)/shard_map/ppermute | solution.py:27
  (22 other events, 107.4 us)
